TPU v7x, 512 devices: a whole 4x8x8 slice. The times are simulated.
512 devices in a mesh: dp: 256 (over x, z, y), cent: 2 (over core).
Axes of the slice: x: 4, y: 8, z: 8, core: 2. Of those that a mesh axis runs over, the one named last changes fastest.
Arguments:
- tokens: float32 [30720, 128], P('dp'), may hold values from -6 to 6
- centroids: float32 [32768, 128], P(('dp', 'cent')), may hold values from -6 to 6
Outputs:
- new_centroids: float32 [32768, 128], P(('dp', 'cent'))
- residuals: float32 [30720, 128], P('dp')
All inputs are finite; a program needn't handle non-finite values.
Results may differ from a plain program's by a relative error of at most 0.0005.
The roundings to bfloat16 on the way count: a program that leaves them out, or rounds other values in their place, can miss the bound.
Values may be sent and summed in bfloat16 or wider, within the bound.
A program may use at most 64 MiB of HBM per device.

v0:
```python
import jax
import jax.numpy as jnp
from jax import lax
from jax.sharding import PartitionSpec as P

ITERS = 3
KB = 2048


EPSILON = 1e-06
SOFTMAX_WARMTH = 0.05


def normalized_rows(values):
    return values * lax.rsqrt(jnp.mean(values * values, axis=-1, keepdims=True) + EPSILON)


def exponent_block(token_half_rows, block):
    affinity_scores = lax.dot_general(
        token_half_rows, block, (((1,), (1,)), ((), ())), preferred_element_type=jnp.float32
    )
    return jnp.exp((affinity_scores / token_half_rows.shape[1] - 1.0) / SOFTMAX_WARMTH)


def shards(tokens, centroids):
    rows_here, feature_dim = tokens.shape
    unit_tok = normalized_rows(tokens)
    token_half_rows = unit_tok.astype(jnp.bfloat16)
    own_rows = normalized_rows(centroids).astype(jnp.bfloat16)
    columns = lax.all_gather(own_rows, "dp", axis=0, tiled=True)
    col_count = columns.shape[0]
    block_count = col_count // KB
    blocks = columns.reshape(block_count, KB, feature_dim)
    col_mass = rows_here * lax.axis_size("dp") / (col_count * lax.axis_size("cent"))
    scales = jnp.ones((block_count, KB), jnp.float32)
    assignment_weight = jnp.ones((rows_here,), jnp.float32)
    for step_index in range(ITERS):

        def row_step(total, packed):
            kernel = exponent_block(token_half_rows, packed[0])
            return (total + jnp.sum(kernel * packed[1][None, :], axis=1), None)

        row_half = lax.scan(row_step, jnp.zeros((rows_here,), jnp.float32), (blocks, scales))[0]
        row_sum = lax.psum(row_half, "cent")
        assignment_weight = 1.0 / row_sum

        def col_only(block):
            kernel = exponent_block(token_half_rows, block)
            return jnp.sum(kernel * assignment_weight[:, None], axis=0)

        col_flat = lax.map(col_only, blocks).reshape(col_count)
        col_total = lax.psum(col_flat, "dp")
        scales = (col_mass / col_total).reshape(block_count, KB)
    weights_bf = assignment_weight.astype(jnp.bfloat16)
    pieces = (
        lax.all_gather(token_half_rows, "dp", axis=0, tiled=True),
        lax.all_gather(weights_bf, "dp", axis=0, tiled=True),
    )
    kernel = exponent_block(pieces[0], own_rows)
    assign_bf = (kernel * pieces[1].astype(jnp.float32)[:, None]).astype(jnp.bfloat16)
    sums_own = lax.dot_general(
        assign_bf, pieces[0], (((0,), (0,)), ((), ())), preferred_element_type=jnp.float32
    )
    new_own = normalized_rows(sums_own)
    fresh = lax.all_gather(new_own.astype(jnp.bfloat16), "dp", axis=0, tiled=True)
    fresh_blocks = fresh.reshape(block_count, KB, feature_dim)

    def soft_step(total, packed):
        kernel = exponent_block(token_half_rows, packed[0])
        transport_plan_half = (kernel * assignment_weight[:, None] * packed[1][None, :]).astype(
            jnp.bfloat16
        )
        return (
            total + jnp.dot(transport_plan_half, packed[2], preferred_element_type=jnp.float32),
            None,
        )

    soft_half = lax.scan(
        soft_step, jnp.zeros((rows_here, feature_dim), jnp.float32), (blocks, scales, fresh_blocks)
    )[0]
    soft = lax.psum(soft_half, "cent")
    return (new_own, unit_tok - soft)


def solution(mesh):
    in_specs = (P("dp", None), P(("dp", "cent"), None))
    out_specs = (P(("dp", "cent"), None), P("dp", None))
    return jax.shard_map(shards, mesh=mesh, in_specs=in_specs, out_specs=out_specs, check_vma=False)
```

profile of v0, /device:TPU:1, one launch (start us, length us, event | category | flops | bytes accessed | tf_op | source)
XLA Modules:
  0.0 2422.9 jit_solution(2898249756367351308)
XLA Ops:
  11.5 130.1 %all-gather.6.cloned.1.call-done = bf16[16384,128]{1,0:T(8,128)(2,1)} async-done(((bf16[64,128]{1,0:T(8,128)(2,1)}), bf16[16384,128]{1,0:T(8,128)(2,1)}) %all-gather.6.cloned.1.call-update) | async-done | bytes 4194320 | tf_op jit(solution)/shard_map/all_gather | solution.py:30
  141.6 13.4 while.91
  141.6 1.6 fusion.131
  143.3 1.6 fusion.131
  145.0 1.6 fusion.131
  146.7 1.6 fusion.131
  148.4 1.6 fusion.131
  150.0 1.6 fusion.131
  151.7 1.6 fusion.131
  153.4 1.6 fusion.131
  155.1 6.3 psum.49
  161.3 14.4 while.88
  163.1 1.6 fusion.122
  164.9 1.6 fusion.122
  168.5 1.6 fusion.122
  173.9 1.6 fusion.122
  176.4 218.9 %all-reduce.5.cloned.1.call-done = f32[16384]{0:T(1024)} async-done(((f32[16384]{0:T(1024)}), f32[16384]{0:T(1024)}) %all-reduce.5.cloned.1.call-update) | async-done | bytes 65552 | tf_op jit(solution)/shard_map/psum | solution.py:52
  396.2 13.7 while.92
  396.3 1.7 fusion.135
  398.0 1.7 fusion.135
  399.7 1.7 fusion.135
  401.4 1.7 fusion.135
  403.1 1.7 fusion.135
  404.8 1.7 fusion.135
  406.5 1.7 fusion.135
  408.3 1.7 fusion.135
  409.9 7.2 psum.51
  417.1 14.4 while.89
  417.1 1.6 fusion.125
  420.7 1.6 fusion.125
  422.5 1.6 fusion.125
  426.1 1.6 fusion.125
  434.8 214.8 %all-reduce.7.cloned.1.call-done = f32[16384]{0:T(1024)} async-done(((f32[16384]{0:T(1024)}), f32[16384]{0:T(1024)}) %all-reduce.7.cloned.1.call-update) | async-done | bytes 65552 | tf_op jit(solution)/shard_map/psum | solution.py:52
  650.4 13.7 while.93
  650.5 1.7 fusion.139
  652.2 1.7 fusion.139
  653.9 1.7 fusion.139
  655.6 1.7 fusion.139
  657.3 1.7 fusion.139
  659.0 1.7 fusion.139
  660.7 1.7 fusion.139
  662.5 1.7 fusion.139
  664.1 7.2 psum.53
  671.6 1146.0 %all-reduce = bf16[30720]{0:T(1024)(128)(2,1)S(1)} all-reduce(bf16[30720]{0:T(1024)(128)(2,1)S(1)} %dynamic-update-slice), channel_id=1, replica_groups=mesh['dp'=256,'cent'=2] {'dp'}, use_global_device_ids=true, to_apply=%add | all-reduce | flops 30720 | bytes 122880
  1817.6 14.4 while.90
  1817.6 1.6 fusion.128
  1821.2 1.6 fusion.128
  1823.0 1.6 fusion.128
  1826.6 1.6 fusion.128
  1828.4 1.6 fusion.128
  1830.2 1.6 fusion.128
  1832.7 9.6 multiply_reduce_fusion.1
  1843.0 421.1 %all-reduce.9.cloned.1.call-done = f32[16384]{0:T(1024)} async-done(((f32[16384]{0:T(1024)}), f32[16384]{0:T(1024)}) %all-reduce.9.cloned.1.call-update) | async-done | bytes 65552 | tf_op jit(solution)/shard_map/psum | solution.py:52
  2265.0 126.2 %all-gather.8.cloned.1.call-done = bf16[16384,128]{1,0:T(8,128)(2,1)} async-done(((bf16[64,128]{1,0:T(8,128)(2,1)}), bf16[16384,128]{1,0:T(8,128)(2,1)}) %all-gather.8.cloned.1.call-update) | async-done | bytes 4194320 | tf_op jit(solution)/shard_map/all_gather | solution.py:65
  2391.2 16.6 while.94
  2391.2 2.0 fusion.144
  2393.3 2.0 fusion.144
  2395.4 2.0 fusion.144
  2397.4 2.0 fusion.144
  2399.5 2.0 fusion.144
  2401.6 2.0 fusion.144
  2403.7 2.0 fusion.144
  2405.7 2.0 fusion.144
  2407.8 7.5 psum.55
  (135 shorter events, 33.7 us)
Async XLA Ops:
  7.2 134.5 %all-gather.6.cloned.1.call-start = ((), (), s32[]{:S(2)}) async-start(), calls=%async_computation.1 | async-start | bytes 4210688 | tf_op jit(solution)/shard_map/all_gather | solution.py:30
  9.6 385.8 %all-reduce.5.cloned.1.call-start = ((), (), s32[]{:S(2)}) async-start(), calls=%async_computation.2 | async-start | bytes 131072 | tf_op jit(solution)/shard_map/psum | solution.py:52
  176.4 473.2 %all-reduce.7.cloned.1.call-start = ((), (), s32[]{:S(2)}) async-start(), calls=%async_computation.3 | async-start | bytes 131072 | tf_op jit(solution)/shard_map/psum | solution.py:52
  431.5 0.7 copy-start.1
  432.2 1400.5 %all-gather.4.cloned.1.call-start = ((), (), s32[]{:S(2)}) async-start(), calls=%async_computation | async-start | bytes 7895040 | tf_op jit(solution)/shard_map/all_gather | solution.py:56
  432.7 1831.4 %all-reduce.9.cloned.1.call-start = ((), (), s32[]{:S(2)}) async-start(), calls=%async_computation.4 | async-start | bytes 131072 | tf_op jit(solution)/shard_map/psum | solution.py:52
  1817.6 15.1 copy-start.3
  1832.6 558.6 %copy-start.2 = (bf16[120,128]{1,0:T(8,128)(2,1)S(1)}, bf16[120,128]{1,0:T(8,128)(2,1)}, u32[]{:S(2)}) copy-start(bf16[120,128]{1,0:T(8,128)(2,1)} %get-tuple-element.1021) | copy-start | bytes 92164
  1832.6 558.6 %all-gather.8.cloned.1.call-start = ((), (), s32[]{:S(2)}) async-start(), calls=%async_computation.5 | async-start | bytes 4210688 | tf_op jit(solution)/shard_map/all_gather | solution.py:65
  2391.2 24.1 copy-start
Sparse Core Ops, SparseCore 0:
  12.9 128.6 all-gather.5
  176.5 218.8 all-reduce.4
  432.3 217.2 all-reduce.6
  654.4 129.2 all-gather.3
  1832.7 431.3 all-reduce.8
  2269.1 122.0 all-gather.7
where the time goes:
time: 2430 us; the launch traced here: 2420 us
  blocking collectives  1170 us (48%)
  waiting for transfers between devices  1110 us (46%)
  matrix products  103 us (4%)
    unnamed x1, blocking collectives  1150 us
    psum x3, waiting for transfers between devices, shards(): col_total = lax.psum(col_flat, 'dp')  855 us
    all_gather x1, waiting for transfers between devices, shards(): columns = lax.all_gather(own_rows, 'dp', axis=0, tiled=True)  130 us
    all_gather x1, waiting for transfers between devices, shards(): lax.all_gather(new_own.astype(jnp.bfloat16), 'dp', axis=0, tiled=True)  126 us
    dot_general x48, matrix products, exponent_block(): lax.dot_general(token_half_rows, block, (((1,), (1,)), ((), ())), preferr...  77.1 us
  transfers between devices with their start and end apart: 6, of which 5 were waited for; matrix products, arithmetic and copies ran while one was open for 2% of the time, Pallas kernels for 0%

commit v1 on v0

v1 whole, which is shorter than its diff:
```python
import functools
import math

import jax
import jax.numpy as jnp
from jax import lax
from jax.experimental import pallas as pl
from jax.experimental.pallas import tpu as pltpu
from jax.sharding import PartitionSpec as P

ITERS = 3
EPSILON = 1e-06
SOFTMAX_WARMTH = 0.05
LANES = 128
HALF = 64
SOFT_CHUNKS = 4
MESH = pl.DeviceIdType.MESH


def layout(dp_size):
    if dp_size == 256:
        return 4, 8, 8, 2, 2
    return 2, 2, dp_size // 4, 1, 1


def normalized_rows(values):
    return values * lax.rsqrt(jnp.mean(values * values, axis=-1, keepdims=True) + EPSILON)


def lane_sums(values):
    total = values[:, :LANES]
    for g in range(1, values.shape[1] // LANES):
        total = total + values[:, g * LANES : (g + 1) * LANES]
    return jnp.sum(total.T, axis=0, keepdims=True)


def fused(
    dims,
    tok_ref,
    cen_ref,
    new_ref,
    res_ref,
    toks,
    toks_t,
    cens,
    kern,
    rows_mine,
    rows_pair,
    rows_in,
    weights,
    weight_cols,
    cols_in,
    cols_out,
    half_mat,
    sums_t,
    sums_out,
    sums_in,
    news,
    soft,
    soft_pair,
    soft_half,
    soft_in,
    soft_fin,
    send_sem,
    recv_sem,
):
    X, Y, Z, BY, BZ = dims
    NB = X * BY * BZ
    NA = (Y // BY) * (Z // BZ)
    rows_here = tok_ref.shape[0]
    width = NA * cen_ref.shape[0]
    groups = width // LANES
    col_mass = (rows_here * X * Y * Z) / (cen_ref.shape[0] * X * Y * Z * 2)

    dp = lax.axis_index("dp")
    core = lax.axis_index("cent")
    y = lax.rem(dp, Y)
    z = lax.rem(lax.div(dp, Y), Z)
    x = lax.div(dp, Y * Z)
    yb, ya = lax.rem(y, BY), lax.div(y, BY)
    zb, za = lax.rem(z, BZ), lax.div(z, BZ)
    AY, AZ = Y // BY, Z // BZ
    sibling = (dp, 1 - core)

    def row_peer(r):
        px = lax.rem(x + r // (BY * BZ), X)
        py = lax.rem(yb + (r // BZ) % BY, BY)
        pz = lax.rem(zb + r % BZ, BZ)
        return (px * Z + za * BZ + pz) * Y + ya * BY + py, (px * BY + py) * BZ + pz

    def col_peer(r):
        py = lax.rem(ya + r // AZ, AY)
        pz = lax.rem(za + r % AZ, AZ)
        return (x * Z + pz * BZ + zb) * Y + py * BY + yb, py * AZ + pz

    row_peers = [row_peer(r) for r in range(NB)]
    col_peers = [col_peer(r) for r in range(NA)]
    mine_b = row_peers[0][1]
    mine_a = col_peers[0][1]
    row_ids = [(p[0], core) for p in row_peers]
    col_ids = [(p[0], core) for p in col_peers]

    barrier = pltpu.get_barrier_semaphore()
    greeted = row_ids[1:] + col_ids[1:] + [sibling]
    for peer in greeted:
        pl.semaphore_signal(barrier, inc=1, device_id=peer, device_id_type=MESH)

    def send(src, dst, phase, peer):
        copy = pltpu.make_async_remote_copy(
            src_ref=src,
            dst_ref=dst,
            send_sem=send_sem.at[phase],
            recv_sem=recv_sem.at[phase],
            device_id=peer,
            device_id_type=MESH,
        )
        copy.start()
        return copy

    def arrived(view, phase):
        pltpu.make_async_copy(view, view, recv_sem.at[phase]).wait()

    sent = []

    def depart(view, phase):
        sent.append((view, phase))

    phases = iter(range(64))

    unit_tok = normalized_rows(tok_ref[...])
    pad = jnp.zeros((LANES - rows_here, LANES), jnp.float32)
    toks[mine_b] = jnp.concatenate([unit_tok, pad], axis=0).astype(jnp.bfloat16)
    cens[mine_a] = normalized_rows(cen_ref[...]).astype(jnp.bfloat16)
    pl.semaphore_wait(barrier, len(greeted))
    tok_phase, cen_phase = next(phases), next(phases)
    for r in range(1, NA):
        send(cens.at[mine_a], cens.at[mine_a], cen_phase, col_ids[r])
    for r in range(1, NB):
        send(toks.at[mine_b], toks.at[mine_b], tok_phase, row_ids[r])
    arrived(cens.at[pl.ds(0, NA - 1)], cen_phase)
    depart(cens.at[pl.ds(0, NA - 1)], cen_phase)
    arrived(toks.at[pl.ds(0, NB - 1)], tok_phase)
    depart(toks.at[pl.ds(0, NB - 1)], tok_phase)

    slope = math.log2(math.e) / (SOFTMAX_WARMTH * LANES)
    offset = math.log2(math.e) / SOFTMAX_WARMTH
    columns = cens[...].reshape(width, LANES)

    def kernel_rows(b, carry):
        affinity = lax.dot_general(
            toks[b], columns, (((1,), (1,)), ((), ())), preferred_element_type=jnp.float32
        )
        kernel = jnp.exp2(affinity * slope - offset)
        kern[b] = kernel
        rows_mine[0, pl.ds(b, 1), :] = lane_sums(kernel)
        return carry

    lax.fori_loop(0, NB, kernel_rows, 0)

    valid = lax.broadcasted_iota(jnp.int32, (NB, LANES), 1) < rows_here
    scales = None
    for it in range(ITERS):
        if it:
            scale_rows = scales

            def scaled_rows(b, carry):
                total = kern[b, :, :LANES] * scale_rows[0:1, :]
                for g in range(1, groups):
                    total = total + kern[b, :, g * LANES : (g + 1) * LANES] * scale_rows[g : g + 1, :]
                rows_mine[it, pl.ds(b, 1), :] = lane_sums(total)
                return carry

            lax.fori_loop(0, NB, scaled_rows, 0)

        phase = next(phases)
        send(rows_mine.at[it], rows_pair.at[it], phase, sibling)
        if it == 0:
            def turn(b, carry):
                toks_t[b] = toks[b].astype(jnp.float32).T.astype(jnp.bfloat16)
                return carry

            lax.fori_loop(0, NB, turn, 0)
        arrived(rows_pair.at[it], phase)
        depart(rows_pair.at[it], phase)
        rows_in[it, 0] = rows_mine[it] + rows_pair[it]
        phase = next(phases)
        for r in range(1, NB):
            send(rows_in.at[it, 0], rows_in.at[it, r], phase, row_ids[r])
        arrived(rows_in.at[it, pl.ds(1, NB - 1)], phase)
        depart(rows_in.at[it, pl.ds(1, NB - 1)], phase)
        row_sum = jnp.sum(rows_in[it], axis=0)
        weights[...] = jnp.where(valid, 1.0 / row_sum, 0.0)

        def weighted_columns(b, totals):
            spread = jnp.broadcast_to(weights[pl.ds(b, 1), :], (LANES, LANES)).T
            weight_cols[b] = spread
            return tuple(
                totals[g]
                + jnp.sum(
                    (kern[b, :, g * LANES : (g + 1) * LANES] * spread).reshape(LANES // 8, 8, LANES), axis=0
                )
                for g in range(groups)
            )

        totals = lax.fori_loop(
            0, NB, weighted_columns, tuple(jnp.zeros((8, LANES), jnp.float32) for _ in range(groups))
        )
        for g in range(groups):
            cols_in[it, 0, g : g + 1, :] = jnp.sum(totals[g], axis=0, keepdims=True)
        col_phase = next(phases)
        for r in range(1, NA):
            send(cols_in.at[it, 0], cols_in.at[it, r], col_phase, col_ids[r])

        if it == ITERS - 1:
            def assign_rows(b, carry):
                spread = weight_cols[b].astype(jnp.bfloat16).astype(jnp.float32)
                for g in range(groups):
                    half_mat[b, :, g * LANES : (g + 1) * LANES] = (
                        kern[b, :, g * LANES : (g + 1) * LANES] * spread
                    ).astype(jnp.bfloat16)
                return carry

            lax.fori_loop(0, NB, assign_rows, 0)
            sums_t[...] = jnp.zeros_like(sums_t)

            def sum_rows(b, carry):
                sums_t[...] += jnp.dot(toks_t[b], half_mat[b], preferred_element_type=jnp.float32)
                return carry

            lax.fori_loop(0, NB, sum_rows, 0)
            per = LANES // cen_ref.shape[0]
            for g in range(groups):
                turned = sums_t[:, g * LANES : (g + 1) * LANES].T
                for part in range(per):
                    sums_out[g * per + part] = turned[part * HALF : (part + 1) * HALF, :]
            sums_phase = next(phases)
            for r in range(1, NA):
                send(sums_out.at[col_peers[r][1]], sums_in.at[r], sums_phase, col_ids[r])
            sums_in[0] = sums_out[mine_a]

        arrived(cols_in.at[it, pl.ds(1, NA - 1)], col_phase)
        depart(cols_in.at[it, pl.ds(1, NA - 1)], col_phase)
        scales = col_mass / jnp.sum(cols_in[it], axis=0)

    arrived(sums_in.at[pl.ds(1, NA - 1)], sums_phase)
    depart(sums_in.at[pl.ds(1, NA - 1)], sums_phase)
    new_own = normalized_rows(jnp.sum(sums_in[...], axis=0))
    new_ref[...] = new_own
    news[mine_a] = new_own.astype(jnp.bfloat16)
    phase = next(phases)
    for r in range(1, NA):
        send(news.at[mine_a], news.at[mine_a], phase, col_ids[r])

    last_scales = scales

    def plan_rows(b, carry):
        spread = weight_cols[b]
        for g in range(groups):
            half_mat[b, :, g * LANES : (g + 1) * LANES] = (
                kern[b, :, g * LANES : (g + 1) * LANES] * spread * last_scales[g : g + 1, :]
            ).astype(jnp.bfloat16)
        return carry

    lax.fori_loop(0, NB, plan_rows, 0)
    arrived(news.at[pl.ds(0, NA - 1)], phase)
    depart(news.at[pl.ds(0, NA - 1)], phase)
    fresh = news[...].reshape(width, LANES)

    chunk = max(NB // SOFT_CHUNKS, 1)
    pair_phases = []
    for first in range(0, NB, chunk):
        for r in range(first, first + chunk):
            block = jnp.dot(half_mat[row_peers[r][1]], fresh, preferred_element_type=jnp.float32)
            soft[0, r] = block[:HALF]
            soft[1, r] = block[HALF:]
        phase = next(phases)
        pair_phases.append(phase)
        send(soft.at[1 - core, pl.ds(first, chunk)], soft_pair.at[pl.ds(first, chunk)], phase, sibling)
    soft_phase = next(phases)
    for first, phase in zip(range(0, NB, chunk), pair_phases):
        arrived(soft_pair.at[pl.ds(first, chunk)], phase)
        depart(soft_pair.at[pl.ds(first, chunk)], phase)
        for r in range(first, first + chunk):
            if r == 0:
                soft_in[0] = soft[core, 0] + soft_pair[0]
            else:
                soft_half[r] = soft[core, r] + soft_pair[r]
                send(soft_half.at[r], soft_in.at[r], soft_phase, row_ids[r])
    arrived(soft_in.at[pl.ds(1, NB - 1)], soft_phase)
    depart(soft_in.at[pl.ds(1, NB - 1)], soft_phase)
    soft_fin[core] = jnp.sum(soft_in[...], axis=0)
    phase = next(phases)
    send(soft_fin.at[core], soft_fin.at[core], phase, sibling)
    arrived(soft_fin.at[0], phase)
    depart(soft_fin.at[0], phase)
    whole = jnp.concatenate([soft_fin[0], soft_fin[1]], axis=0)
    res_ref[...] = normalized_rows(tok_ref[...]) - whole[:rows_here, :]
    for view, used in sent:
        pltpu.make_async_copy(view, view, send_sem.at[used]).wait()


def shards(dims, tokens, centroids):
    X, Y, Z, BY, BZ = dims
    NB = X * BY * BZ
    NA = (Y // BY) * (Z // BZ)
    width = NA * centroids.shape[0]
    groups = width // LANES
    f32, bf16 = jnp.float32, jnp.bfloat16
    scratch = [
        pltpu.VMEM((NB, LANES, LANES), bf16),
        pltpu.VMEM((NB, LANES, LANES), bf16),
        pltpu.VMEM((NA, HALF, LANES), bf16),
        pltpu.VMEM((NB, LANES, width), f32),
        pltpu.VMEM((ITERS, NB, LANES), f32),
        pltpu.VMEM((ITERS, NB, LANES), f32),
        pltpu.VMEM((ITERS, NB, NB, LANES), f32),
        pltpu.VMEM((NB, LANES), f32),
        pltpu.VMEM((NB, LANES, LANES), f32),
        pltpu.VMEM((ITERS, NA, groups, LANES), f32),
        pltpu.VMEM((8, LANES), f32),
        pltpu.VMEM((NB, LANES, width), bf16),
        pltpu.VMEM((LANES, width), f32),
        pltpu.VMEM((NA, HALF, LANES), f32),
        pltpu.VMEM((NA, HALF, LANES), f32),
        pltpu.VMEM((NA, HALF, LANES), bf16),
        pltpu.VMEM((2, NB, HALF, LANES), f32),
        pltpu.VMEM((NB, HALF, LANES), f32),
        pltpu.VMEM((NB, HALF, LANES), f32),
        pltpu.VMEM((NB, HALF, LANES), f32),
        pltpu.VMEM((2, HALF, LANES), f32),
        pltpu.SemaphoreType.DMA((24,)),
        pltpu.SemaphoreType.DMA((24,)),
    ]
    return pl.pallas_call(
        functools.partial(fused, dims),
        out_shape=(
            jax.ShapeDtypeStruct(centroids.shape, f32),
            jax.ShapeDtypeStruct(tokens.shape, f32),
        ),
        in_specs=[pl.BlockSpec(memory_space=pltpu.VMEM)] * 2,
        out_specs=[pl.BlockSpec(memory_space=pltpu.VMEM)] * 2,
        scratch_shapes=scratch,
        compiler_params=pltpu.CompilerParams(
            collective_id=0, has_side_effects=True, vmem_limit_bytes=48 * 1024 * 1024
        ),
        name="kmeans_step",
    )(tokens, centroids)


def solution(mesh):
    in_specs = (P("dp", None), P(("dp", "cent"), None))
    out_specs = (P(("dp", "cent"), None), P("dp", None))
    dims = layout(mesh.shape["dp"])
    return jax.shard_map(
        functools.partial(shards, dims), mesh=mesh, in_specs=in_specs, out_specs=out_specs, check_vma=False
    )
```

time: 2430 us -> 124 us (0.05)
  blocking collectives: 1170 us -> 0 us
  waiting for transfers between devices: 1110 us -> 0 us
  Pallas kernels: 0 us -> 121 us
  matrix products: 103 us -> 0 us
    unnamed x1 -> x0, blocking collectives: 1150 us -> none
    psum x3 -> x0, waiting for transfers between devices: 855 us -> none  [shards(): col_total = lax.psum(col_flat, 'dp')]
    all_gather x3 -> x0, waiting for transfers between devices: 256 us -> none  [the longest x1 130 us: shards(): columns = lax.all_gather(own_rows, 'dp', axis=0, tiled=True)]
    pallas_call x0 -> x1, Pallas kernels: none -> 121 us  [shards(): pl.pallas_call(functools.partial(fused, dims), out_shape=(jax.ShapeDtypeS...]
    dot_general x57 -> x0, matrix products: 103 us -> none  [the longest x48 77.1 us: exponent_block(): lax.dot_general(token_half_rows, block, (((1,), (1,)), ((), ())), preferr...]
    psum x4 -> x0, blocking collectives: 28.1 us -> none  [the longest x3 20.6 us: shards(): row_sum = lax.psum(row_half, 'cent')]
  transfers between devices with their start and end apart: 6 -> 0, of which waited for: 5 -> 0; matrix products, arithmetic and copies ran while one was open for 2% -> 0% of each run, Pallas kernels for 0% -> 0%
where the time goes in v1:
time: 124 us
  Pallas kernels  121 us (98%)
  local copies, waits for them, and re-layouts  2.82 us (2%)
    pallas_call x1, Pallas kernels, shards(): pl.pallas_call(functools.partial(fused, dims), out_shape=(jax.ShapeDtypeS...  121 us
    unnamed x6, local copies, waits for them, and re-layouts  2.82 us

profile of v1, /device:TPU:1, one launch (start us, length us, event | category | flops | bytes accessed | tf_op | source)
XLA Modules:
  0.0 124.1 jit_solution(3844443183902143913)
XLA Ops:
  0.6 0.0 copy-start
  0.6 0.8 copy-done
  1.5 0.0 copy-start.1
  1.5 0.8 copy-done.1
  2.2 120.7 %kmeans_step.1 = (f32[64,128]{1,0:T(8,128)S(1)}, f32[120,128]{1,0:T(8,128)S(1)}) custom-call(f32[120,128]{1,0:T(8,128)S(1)} %copy-done, f32[64,128]{1,0:T(8,128)S(1)} %copy-done.1), custom_call_target="tpu_custom_call" | custom-call | tf_op jit(solution)/shard_map/kmeans_step/pallas_call | solution.py:334
  122.9 0.6 copy.6
  123.5 0.6 copy.7
Async XLA Ops:
  0.6 0.8 copy-start
  1.5 0.8 copy-start.1

commit v2 on v1

v2 whole, which is shorter than its diff:
```python
import functools
import math

import jax
import jax.numpy as jnp
from jax import lax
from jax.experimental import pallas as pl
from jax.experimental.pallas import tpu as pltpu
from jax.sharding import PartitionSpec as P

ITERS = 3
EPSILON = 1e-06
SOFTMAX_WARMTH = 0.05
LANES = 128
HALF = 64
SOFT_CHUNKS = 4
MESH = pl.DeviceIdType.MESH


def layout(dp_size):
    if dp_size == 256:
        return 4, 8, 8, 2, 2
    return 2, 2, dp_size // 4, 1, 1


def nearest_first(size):
    return sorted(range(size), key=lambda step: min(step, size - step))


def normalized_rows(values):
    return values * lax.rsqrt(jnp.mean(values * values, axis=-1, keepdims=True) + EPSILON)


def lane_sums(values):
    total = values[:, :LANES]
    for g in range(1, values.shape[1] // LANES):
        total = total + values[:, g * LANES : (g + 1) * LANES]
    return jnp.sum(total.T, axis=0, keepdims=True)


def fused(
    dims,
    tok_ref,
    cen_ref,
    new_ref,
    res_ref,
    toks,
    toks_t,
    cens,
    kern,
    tile_acc,
    rows_mine,
    rows_pair,
    rows_in,
    weights,
    weight_cols,
    cols_in,
    half_mat,
    sums_out,
    sums_in,
    news,
    soft,
    soft_pair,
    soft_half,
    soft_in,
    soft_fin,
    send_sem,
    recv_sem,
):
    X, Y, Z, BY, BZ = dims
    AY, AZ = Y // BY, Z // BZ
    NB, NA = X * BY * BZ, AY * AZ
    rows_here = tok_ref.shape[0]
    panel = AZ * HALF
    groups = NA * HALF // LANES
    per_panel = panel // LANES
    many = min(NB, 4)
    col_mass = (rows_here * X * Y * Z) / (HALF * X * Y * Z * 2)

    dp = lax.axis_index("dp")
    core = lax.axis_index("cent")
    y = lax.rem(dp, Y)
    z = lax.rem(lax.div(dp, Y), Z)
    x = lax.div(dp, Y * Z)
    yb, ya = lax.rem(y, BY), lax.div(y, BY)
    zb, za = lax.rem(z, BZ), lax.div(z, BZ)
    sibling = (dp, 1 - core)

    def row_peer(r):
        px = lax.rem(x + r // (BY * BZ), X)
        py = lax.rem(yb + (r // BZ) % BY, BY)
        pz = lax.rem(zb + r % BZ, BZ)
        return (px * Z + za * BZ + pz) * Y + ya * BY + py, (px * BY + py) * BZ + pz

    def col_peer(r):
        py = lax.rem(ya + r // AZ, AY)
        pz = lax.rem(za + r % AZ, AZ)
        return (x * Z + pz * BZ + zb) * Y + py * BY + yb, py * AZ + pz

    row_peers = [row_peer(r) for r in range(NB)]
    col_peers = [col_peer(r) for r in range(NA)]
    mine_b = row_peers[0][1]
    mine_a = col_peers[0][1]
    row_ids = [(p[0], core) for p in row_peers]
    col_ids = [(p[0], core) for p in col_peers]
    steps = nearest_first(AY)
    panel_at = [lax.rem(ya + (AY - step) % AY, AY) for step in range(AY)]
    far_first = [step * AZ + other for step in reversed(steps) for other in reversed(nearest_first(AZ))]

    barrier = pltpu.get_barrier_semaphore()
    greeted = row_ids[1:] + col_ids[1:] + [sibling]
    for peer in greeted:
        pl.semaphore_signal(barrier, inc=1, device_id=peer, device_id_type=MESH)

    def send(src, dst, phase, peer):
        pltpu.make_async_remote_copy(
            src_ref=src,
            dst_ref=dst,
            send_sem=send_sem.at[phase],
            recv_sem=recv_sem.at[phase],
            device_id=peer,
            device_id_type=MESH,
        ).start()

    sent = []

    def arrived(view, phase):
        pltpu.make_async_copy(view, view, recv_sem.at[phase]).wait()
        sent.append((view, phase))

    phases = iter(range(32))

    def slot(b):
        return jnp.concatenate([toks[0, b], toks[1, b]], axis=0)

    pad = jnp.zeros((LANES - rows_here, LANES), jnp.float32)
    unit_tok = jnp.concatenate([normalized_rows(tok_ref[...]), pad], axis=0)
    toks[core, mine_b] = jnp.where(core == 0, unit_tok[:HALF], unit_tok[HALF:]).astype(jnp.bfloat16)
    cens[mine_a] = normalized_rows(cen_ref[...]).astype(jnp.bfloat16)
    pl.semaphore_wait(barrier, len(greeted))
    tok_phase, pair_phase = next(phases), next(phases)
    cen_phases = [next(phases) for _ in range(AY)]
    for r in range(1, NB):
        send(toks.at[core, mine_b], toks.at[core, mine_b], tok_phase, row_ids[r])
    for step in steps:
        for r in range(step * AZ, step * AZ + AZ):
            if r:
                send(cens.at[mine_a], cens.at[mine_a], cen_phases[step], col_ids[r])
    arrived(toks.at[0, pl.ds(0, NB - 1)], tok_phase)
    send(toks.at[core], toks.at[core], pair_phase, sibling)
    arrived(toks.at[0], pair_phase)

    slope = math.log2(math.e) / (SOFTMAX_WARMTH * LANES)
    offset = math.log2(math.e) / SOFTMAX_WARMTH
    for order, step in enumerate(steps):
        at = panel_at[step]
        arrived(cens.at[pl.ds(0, AZ - (step == 0))], cen_phases[step])
        columns = cens[pl.ds(at * AZ, AZ)].reshape(panel, LANES)

        def kernel_rows(i, carry):
            first = i * many
            block = jnp.concatenate([slot(first + j) for j in range(many)], axis=0)
            affinity = lax.dot_general(
                block, columns, (((1,), (1,)), ((), ())), preferred_element_type=jnp.float32
            )
            kernel = jnp.exp2(affinity * slope - offset)
            for j in range(many):
                part = kernel[j * LANES : (j + 1) * LANES]
                kern[at, first + j] = part
                total = part[:, :LANES]
                for h in range(1, per_panel):
                    total = total + part[:, h * LANES : (h + 1) * LANES]
                if order:
                    total = total + tile_acc[first + j]
                if order < AY - 1:
                    tile_acc[first + j] = total
                else:
                    rows_mine[0, pl.ds(first + j, 1), :] = jnp.sum(total.T, axis=0, keepdims=True)
            return carry

        lax.fori_loop(0, NB // many, kernel_rows, 0)

    def part_of(b, g):
        h = g % per_panel
        return kern[g // per_panel, b, :, h * LANES : (h + 1) * LANES]

    valid = lax.broadcasted_iota(jnp.int32, (NB, LANES), 1) < rows_here
    scales = None
    for it in range(ITERS):
        if it:
            scale_rows = scales

            def scaled_rows(b, carry):
                total = part_of(b, 0) * scale_rows[0:1, :]
                for g in range(1, groups):
                    total = total + part_of(b, g) * scale_rows[g : g + 1, :]
                rows_mine[it, pl.ds(b, 1), :] = jnp.sum(total.T, axis=0, keepdims=True)
                return carry

            lax.fori_loop(0, NB, scaled_rows, 0, unroll=many)

        phase = next(phases)
        send(rows_mine.at[it], rows_pair.at[it], phase, sibling)
        arrived(rows_pair.at[it], phase)
        rows_in[it, 0] = rows_mine[it] + rows_pair[it]
        phase = next(phases)
        for r in range(1, NB):
            send(rows_in.at[it, 0], rows_in.at[it, r], phase, row_ids[r])
        if it == 0:
            def turn(b, carry):
                place = pl.ds(pl.multiple_of(b * LANES, LANES), LANES)
                toks_t[:, place] = slot(b).astype(jnp.float32).T.astype(jnp.bfloat16)
                return carry

            lax.fori_loop(0, NB, turn, 0, unroll=many)
        arrived(rows_in.at[it, pl.ds(1, NB - 1)], phase)
        row_sum = jnp.sum(rows_in[it], axis=0)
        weights[...] = jnp.where(valid, 1.0 / row_sum, 0.0)

        def weighted_columns(b, totals):
            spread = jnp.broadcast_to(weights[pl.ds(b, 1), :], (LANES, LANES)).T
            weight_cols[b] = spread
            return tuple(
                totals[g] + jnp.sum((part_of(b, g) * spread).reshape(LANES // 8, 8, LANES), axis=0)
                for g in range(groups)
            )

        zeros = tuple(jnp.zeros((8, LANES), jnp.float32) for _ in range(groups))
        totals = lax.fori_loop(0, NB, weighted_columns, zeros, unroll=many)
        for g in range(groups):
            cols_in[it, 0, g : g + 1, :] = jnp.sum(totals[g], axis=0, keepdims=True)
        col_phase = next(phases)
        for r in far_first:
            if r:
                send(cols_in.at[it, 0], cols_in.at[it, r], col_phase, col_ids[r])

        if it == ITERS - 1:
            sums_phase = next(phases)
            for step in reversed(steps):
                at = lax.rem(ya + step, AY)

                def assign_rows(b, carry):
                    spread = weight_cols[b].astype(jnp.bfloat16).astype(jnp.float32)
                    for h in range(per_panel):
                        lanes = slice(h * LANES, (h + 1) * LANES)
                        half_mat[step, b, :, lanes] = (kern[at, b, :, lanes] * spread).astype(jnp.bfloat16)
                    return carry

                lax.fori_loop(0, NB, assign_rows, 0, unroll=many)
                turned = jnp.dot(
                    toks_t[...],
                    half_mat[step].reshape(NB * LANES, panel),
                    preferred_element_type=jnp.float32,
                )
                for h in range(per_panel):
                    pair = turned[:, h * LANES : (h + 1) * LANES].T
                    sums_out[at * AZ + 2 * h] = pair[:HALF]
                    sums_out[at * AZ + 2 * h + 1] = pair[HALF:]
                for r in far_first:
                    if r and r // AZ == step:
                        send(sums_out.at[col_peers[r][1]], sums_in.at[r], sums_phase, col_ids[r])
            sums_in[0] = sums_out[mine_a]

        arrived(cols_in.at[it, pl.ds(1, NA - 1)], col_phase)
        scales = col_mass / jnp.sum(cols_in[it], axis=0)

    last_scales = scales

    def plan_rows(b, carry):
        spread = weight_cols[b]
        for g in range(groups):
            h = g % per_panel
            half_mat[g // per_panel, b, :, h * LANES : (h + 1) * LANES] = (
                part_of(b, g) * spread * last_scales[g : g + 1, :]
            ).astype(jnp.bfloat16)
        return carry

    lax.fori_loop(0, NB, plan_rows, 0, unroll=many)

    arrived(sums_in.at[pl.ds(1, NA - 1)], sums_phase)
    new_own = normalized_rows(jnp.sum(sums_in[...], axis=0))
    news[mine_a] = new_own.astype(jnp.bfloat16)
    new_phases = [next(phases) for _ in range(AY)]
    for r in far_first:
        if r:
            send(news.at[mine_a], news.at[mine_a], new_phases[r // AZ], col_ids[r])
    new_ref[...] = new_own

    chunk = max(NB // SOFT_CHUNKS, 1)
    soft_phases = []
    for order, step in enumerate(steps):
        at = panel_at[step]
        arrived(news.at[pl.ds(0, AZ - (step == 0))], new_phases[step])
        fresh = news[pl.ds(at * AZ, AZ)].reshape(panel, LANES)
        if order < AY - 1:

            def soft_rows(i, carry):
                place = pl.ds(i * many, many)
                block = jnp.dot(
                    half_mat[at, place].reshape(many * LANES, panel), fresh, preferred_element_type=jnp.float32
                ).reshape(many, LANES, LANES)
                tile_acc[place] = block if order == 0 else tile_acc[place] + block
                return carry

            lax.fori_loop(0, NB // many, soft_rows, 0)
            continue
        for first in range(0, NB, chunk):
            block = jnp.dot(
                jnp.concatenate([half_mat[at, row_peers[r][1]] for r in range(first, first + chunk)], axis=0),
                fresh,
                preferred_element_type=jnp.float32,
            )
            for r in range(first, first + chunk):
                whole = block[(r - first) * LANES : (r - first + 1) * LANES] + tile_acc[row_peers[r][1]]
                soft[0, r] = whole[:HALF]
                soft[1, r] = whole[HALF:]
            phase = next(phases)
            soft_phases.append(phase)
            send(soft.at[1 - core, pl.ds(first, chunk)], soft_pair.at[pl.ds(first, chunk)], phase, sibling)
    soft_phase = next(phases)
    for first, phase in zip(range(0, NB, chunk), soft_phases):
        arrived(soft_pair.at[pl.ds(first, chunk)], phase)
        for r in range(first, first + chunk):
            if r == 0:
                soft_in[0] = soft[core, 0] + soft_pair[0]
            else:
                soft_half[r] = soft[core, r] + soft_pair[r]
                send(soft_half.at[r], soft_in.at[r], soft_phase, row_ids[r])
    arrived(soft_in.at[pl.ds(1, NB - 1)], soft_phase)
    soft_fin[core] = jnp.sum(soft_in[...], axis=0)
    phase = next(phases)
    send(soft_fin.at[core], soft_fin.at[core], phase, sibling)
    unit_tok = normalized_rows(tok_ref[...])
    arrived(soft_fin.at[0], phase)
    whole = jnp.concatenate([soft_fin[0], soft_fin[1]], axis=0)
    res_ref[...] = unit_tok - whole[:rows_here, :]
    for view, used in sent:
        pltpu.make_async_copy(view, view, send_sem.at[used]).wait()


def shards(dims, tokens, centroids):
    X, Y, Z, BY, BZ = dims
    AY, AZ = Y // BY, Z // BZ
    NB, NA = X * BY * BZ, AY * AZ
    panel = AZ * HALF
    groups = NA * HALF // LANES
    f32, bf16 = jnp.float32, jnp.bfloat16
    scratch = [
        pltpu.VMEM((2, NB, HALF, LANES), bf16),
        pltpu.VMEM((LANES, NB * LANES), bf16),
        pltpu.VMEM((NA, HALF, LANES), bf16),
        pltpu.VMEM((AY, NB, LANES, panel), f32),
        pltpu.VMEM((NB, LANES, LANES), f32),
        pltpu.VMEM((ITERS, NB, LANES), f32),
        pltpu.VMEM((ITERS, NB, LANES), f32),
        pltpu.VMEM((ITERS, NB, NB, LANES), f32),
        pltpu.VMEM((NB, LANES), f32),
        pltpu.VMEM((NB, LANES, LANES), f32),
        pltpu.VMEM((ITERS, NA, groups, LANES), f32),
        pltpu.VMEM((AY, NB, LANES, panel), bf16),
        pltpu.VMEM((NA, HALF, LANES), f32),
        pltpu.VMEM((NA, HALF, LANES), f32),
        pltpu.VMEM((NA, HALF, LANES), bf16),
        pltpu.VMEM((2, NB, HALF, LANES), f32),
        pltpu.VMEM((NB, HALF, LANES), f32),
        pltpu.VMEM((NB, HALF, LANES), f32),
        pltpu.VMEM((NB, HALF, LANES), f32),
        pltpu.VMEM((2, HALF, LANES), f32),
        pltpu.SemaphoreType.DMA((32,)),
        pltpu.SemaphoreType.DMA((32,)),
    ]
    return pl.pallas_call(
        functools.partial(fused, dims),
        out_shape=(
            jax.ShapeDtypeStruct(centroids.shape, f32),
            jax.ShapeDtypeStruct(tokens.shape, f32),
        ),
        in_specs=[pl.BlockSpec(memory_space=pltpu.VMEM)] * 2,
        out_specs=[pl.BlockSpec(memory_space=pltpu.VMEM)] * 2,
        scratch_shapes=scratch,
        compiler_params=pltpu.CompilerParams(
            collective_id=0, has_side_effects=True, vmem_limit_bytes=48 * 1024 * 1024
        ),
        name="kmeans_step",
    )(tokens, centroids)


def solution(mesh):
    in_specs = (P("dp", None), P(("dp", "cent"), None))
    out_specs = (P(("dp", "cent"), None), P("dp", None))
    dims = layout(mesh.shape["dp"])
    return jax.shard_map(
        functools.partial(shards, dims), mesh=mesh, in_specs=in_specs, out_specs=out_specs, check_vma=False
    )
```

time: 124 us -> 113 us (0.911)
  Pallas kernels: 121 us -> 109 us
    pallas_call x1, Pallas kernels: 121 us -> 109 us  [shards(): pl.pallas_call(functools.partial(fused, dims), out_shape=(jax.ShapeDtypeS...]
where the time goes in v2:
time: 113 us
  Pallas kernels  109 us (96%)
  local copies, waits for them, and re-layouts  2.82 us (2%)
    pallas_call x1, Pallas kernels, shards(): pl.pallas_call(functools.partial(fused, dims), out_shape=(jax.ShapeDtypeS...  109 us
    unnamed x6, local copies, waits for them, and re-layouts  2.82 us

profile of v2, /device:TPU:1, one launch (start us, length us, event | category | flops | bytes accessed | tf_op | source)
XLA Modules:
  0.0 112.6 jit_solution(11579358902765180817)
XLA Ops:
  0.6 0.0 copy-start
  0.6 0.8 copy-done
  1.5 0.0 copy-start.1
  1.5 0.8 copy-done.1
  2.2 109.2 %kmeans_step.1 = (f32[64,128]{1,0:T(8,128)S(1)}, f32[120,128]{1,0:T(8,128)S(1)}) custom-call(f32[120,128]{1,0:T(8,128)S(1)} %copy-done, f32[64,128]{1,0:T(8,128)S(1)} %copy-done.1), custom_call_target="tpu_custom_call" | custom-call | tf_op jit(solution)/shard_map/kmeans_step/pallas_call | solution.py:372
  111.4 0.6 copy.6
  112.0 0.6 copy.7
Async XLA Ops:
  0.6 0.8 copy-start
  1.5 0.8 copy-start.1

commit v3 on v2

--- a/solution.py
+++ b/solution.py
@@ -40,10 +40,12 @@
 
 def fused(
     dims,
+    tok_hbm,
+    cen_hbm,
+    new_ref,
+    res_ref,
     tok_ref,
     cen_ref,
-    new_ref,
-    res_ref,
     toks,
     toks_t,
     cens,
@@ -66,11 +68,16 @@
     soft_fin,
     send_sem,
     recv_sem,
+    load_sem,
 ):
     X, Y, Z, BY, BZ = dims
     AY, AZ = Y // BY, Z // BZ
     NB, NA = X * BY * BZ, AY * AZ
     rows_here = tok_ref.shape[0]
+    load_tok = pltpu.make_async_copy(tok_hbm, tok_ref, load_sem.at[0])
+    load_cen = pltpu.make_async_copy(cen_hbm, cen_ref, load_sem.at[1])
+    load_tok.start()
+    load_cen.start()
     panel = AZ * HALF
     groups = NA * HALF // LANES
     per_panel = panel // LANES
@@ -108,7 +115,9 @@
     far_first = [step * AZ + other for step in reversed(steps) for other in reversed(nearest_first(AZ))]
 
     barrier = pltpu.get_barrier_semaphore()
-    greeted = row_ids[1:] + col_ids[1:] + [sibling]
+    along_z = [r for r in nearest_first(AZ) if r]
+    along_y = [step * AZ for step in steps if step]
+    greeted = row_ids[1:] + [col_ids[r] for r in along_z + along_y] + [sibling]
     for peer in greeted:
         pl.semaphore_signal(barrier, inc=1, device_id=peer, device_id_type=MESH)
 
@@ -128,24 +137,32 @@
         pltpu.make_async_copy(view, view, recv_sem.at[phase]).wait()
         sent.append((view, phase))
 
-    phases = iter(range(32))
+    phases = iter(range(48))
 
     def slot(b):
         return jnp.concatenate([toks[0, b], toks[1, b]], axis=0)
 
+    load_tok.wait()
+    load_cen.wait()
     pad = jnp.zeros((LANES - rows_here, LANES), jnp.float32)
     unit_tok = jnp.concatenate([normalized_rows(tok_ref[...]), pad], axis=0)
     toks[core, mine_b] = jnp.where(core == 0, unit_tok[:HALF], unit_tok[HALF:]).astype(jnp.bfloat16)
     cens[mine_a] = normalized_rows(cen_ref[...]).astype(jnp.bfloat16)
     pl.semaphore_wait(barrier, len(greeted))
     tok_phase, pair_phase = next(phases), next(phases)
+    z_phases = [next(phases) for _ in range(AZ)]
     cen_phases = [next(phases) for _ in range(AY)]
+    for r in reversed(along_z):
+        send(cens.at[mine_a], cens.at[mine_a], z_phases[r], col_ids[r])
+    for r in reversed(along_y):
+        send(cens.at[mine_a], cens.at[mine_a], cen_phases[r // AZ], col_ids[r])
     for r in range(1, NB):
         send(toks.at[core, mine_b], toks.at[core, mine_b], tok_phase, row_ids[r])
-    for step in steps:
-        for r in range(step * AZ, step * AZ + AZ):
-            if r:
-                send(cens.at[mine_a], cens.at[mine_a], cen_phases[step], col_ids[r])
+    for step in along_z:
+        piece = ya * AZ + lax.rem(za + AZ - step, AZ)
+        arrived(cens.at[0], z_phases[step])
+        for r in reversed(along_y):
+            send(cens.at[piece], cens.at[piece], cen_phases[r // AZ], col_ids[r])
     arrived(toks.at[0, pl.ds(0, NB - 1)], tok_phase)
     send(toks.at[core], toks.at[core], pair_phase, sibling)
     arrived(toks.at[0], pair_phase)
@@ -154,7 +171,8 @@
     offset = math.log2(math.e) / SOFTMAX_WARMTH
     for order, step in enumerate(steps):
         at = panel_at[step]
-        arrived(cens.at[pl.ds(0, AZ - (step == 0))], cen_phases[step])
+        if step:
+            arrived(cens.at[pl.ds(0, AZ)], cen_phases[step])
         columns = cens[pl.ds(at * AZ, AZ)].reshape(panel, LANES)
 
         def kernel_rows(i, carry):
@@ -346,6 +364,8 @@
     groups = NA * HALF // LANES
     f32, bf16 = jnp.float32, jnp.bfloat16
     scratch = [
+        pltpu.VMEM(tokens.shape, f32),
+        pltpu.VMEM(centroids.shape, f32),
         pltpu.VMEM((2, NB, HALF, LANES), bf16),
         pltpu.VMEM((LANES, NB * LANES), bf16),
         pltpu.VMEM((NA, HALF, LANES), bf16),
@@ -366,8 +386,9 @@
         pltpu.VMEM((NB, HALF, LANES), f32),
         pltpu.VMEM((NB, HALF, LANES), f32),
         pltpu.VMEM((2, HALF, LANES), f32),
-        pltpu.SemaphoreType.DMA((32,)),
-        pltpu.SemaphoreType.DMA((32,)),
+        pltpu.SemaphoreType.DMA((48,)),
+        pltpu.SemaphoreType.DMA((48,)),
+        pltpu.SemaphoreType.DMA((2,)),
     ]
     return pl.pallas_call(
         functools.partial(fused, dims),
@@ -375,7 +396,7 @@
             jax.ShapeDtypeStruct(centroids.shape, f32),
             jax.ShapeDtypeStruct(tokens.shape, f32),
         ),
-        in_specs=[pl.BlockSpec(memory_space=pltpu.VMEM)] * 2,
+        in_specs=[pl.BlockSpec(memory_space=pl.ANY)] * 2,
         out_specs=[pl.BlockSpec(memory_space=pltpu.VMEM)] * 2,
         scratch_shapes=scratch,
         compiler_params=pltpu.CompilerParams(

time: 113 us -> 111 us (0.982)
  Pallas kernels: 109 us -> 107 us
    pallas_call x1, Pallas kernels: 109 us -> 107 us  [shards(): pl.pallas_call(functools.partial(fused, dims), out_shape=(jax.ShapeDtypeS...]
where the time goes in v3:
time: 111 us; the launch traced here: 110 us
  Pallas kernels  107 us (96%)
  local copies, waits for them, and re-layouts  2.82 us (3%)
    pallas_call x1, Pallas kernels, shards(): pl.pallas_call(functools.partial(fused, dims), out_shape=(jax.ShapeDtypeS...  107 us
    unnamed x6, local copies, waits for them, and re-layouts  2.82 us

profile of v3, /device:TPU:1, one launch (start us, length us, event | category | flops | bytes accessed | tf_op | source)
XLA Modules:
  0.0 110.4 jit_solution(16050968261778162213)
XLA Ops:
  0.6 0.0 copy-start
  0.6 0.8 copy-done
  1.5 0.0 copy-start.1
  1.5 0.8 copy-done.1
  2.2 106.9 %kmeans_step.1 = (f32[64,128]{1,0:T(8,128)S(1)}, f32[120,128]{1,0:T(8,128)S(1)}) custom-call(f32[120,128]{1,0:T(8,128)S(1)} %copy-done, f32[64,128]{1,0:T(8,128)S(1)} %copy-done.1), custom_call_target="tpu_custom_call" | custom-call | tf_op jit(solution)/shard_map/kmeans_step/pallas_call | solution.py:393
  109.1 0.6 copy.6
  109.7 0.6 copy.7
Async XLA Ops:
  0.6 0.8 copy-start
  1.5 0.8 copy-start.1

commit v4 on v3

--- a/solution.py
+++ b/solution.py
@@ -13,6 +13,7 @@
 SOFTMAX_WARMTH = 0.05
 LANES = 128
 HALF = 64
+QUARTER = 32
 SOFT_CHUNKS = 4
 MESH = pl.DeviceIdType.MESH
 
@@ -114,6 +115,9 @@
     panel_at = [lax.rem(ya + (AY - step) % AY, AY) for step in range(AY)]
     far_first = [step * AZ + other for step in reversed(steps) for other in reversed(nearest_first(AZ))]
 
+    span = BY * BZ
+    row_far = [step * span + other for step in reversed(nearest_first(X)) for other in reversed(range(span))]
+
     barrier = pltpu.get_barrier_semaphore()
     along_z = [r for r in nearest_first(AZ) if r]
     along_y = [step * AZ for step in steps if step]
@@ -137,7 +141,7 @@
         pltpu.make_async_copy(view, view, recv_sem.at[phase]).wait()
         sent.append((view, phase))
 
-    phases = iter(range(48))
+    phases = iter(range(56))
 
     def slot(b):
         return jnp.concatenate([toks[0, b], toks[1, b]], axis=0)
@@ -151,18 +155,29 @@
     pl.semaphore_wait(barrier, len(greeted))
     tok_phase, pair_phase = next(phases), next(phases)
     z_phases = [next(phases) for _ in range(AZ)]
+    y_phases = [next(phases) for _ in range(AY)]
     cen_phases = [next(phases) for _ in range(AY)]
+    cross_phases = [next(phases) for _ in range(AY)]
     for r in reversed(along_z):
         send(cens.at[mine_a], cens.at[mine_a], z_phases[r], col_ids[r])
     for r in reversed(along_y):
-        send(cens.at[mine_a], cens.at[mine_a], cen_phases[r // AZ], col_ids[r])
-    for r in range(1, NB):
+        send(cens.at[mine_a], cens.at[mine_a], y_phases[r // AZ], col_ids[r])
+    for r in row_far[:-1]:
         send(toks.at[core, mine_b], toks.at[core, mine_b], tok_phase, row_ids[r])
-    for step in along_z:
-        piece = ya * AZ + lax.rem(za + AZ - step, AZ)
-        arrived(cens.at[0], z_phases[step])
-        for r in reversed(along_y):
-            send(cens.at[piece], cens.at[piece], cen_phases[r // AZ], col_ids[r])
+    low, high = pl.ds(0, QUARTER), pl.ds(QUARTER, QUARTER)
+    for turn_of in range(max(AY, AZ) - 1):
+        if turn_of < AZ - 1:
+            step = along_z[turn_of]
+            piece = ya * AZ + lax.rem(za + AZ - step, AZ)
+            arrived(cens.at[0], z_phases[step])
+            for r in reversed(along_y):
+                send(cens.at[piece, low], cens.at[piece, low], cen_phases[r // AZ], col_ids[r])
+        if turn_of < AY - 1:
+            step = along_y[turn_of] // AZ
+            piece = panel_at[step] * AZ + za
+            arrived(cens.at[0], y_phases[step])
+            for r in reversed(along_z):
+                send(cens.at[piece, high], cens.at[piece, high], cross_phases[step], col_ids[r])
     arrived(toks.at[0, pl.ds(0, NB - 1)], tok_phase)
     send(toks.at[core], toks.at[core], pair_phase, sibling)
     arrived(toks.at[0], pair_phase)
@@ -172,7 +187,8 @@
     for order, step in enumerate(steps):
         at = panel_at[step]
         if step:
-            arrived(cens.at[pl.ds(0, AZ)], cen_phases[step])
+            arrived(cens.at[pl.ds(0, AZ - 1), low], cen_phases[step])
+            arrived(cens.at[pl.ds(0, AZ - 1), high], cross_phases[step])
         columns = cens[pl.ds(at * AZ, AZ)].reshape(panel, LANES)
 
         def kernel_rows(i, carry):
@@ -222,7 +238,7 @@
         arrived(rows_pair.at[it], phase)
         rows_in[it, 0] = rows_mine[it] + rows_pair[it]
         phase = next(phases)
-        for r in range(1, NB):
+        for r in row_far[:-1]:
             send(rows_in.at[it, 0], rows_in.at[it, r], phase, row_ids[r])
         if it == 0:
             def turn(b, carry):
@@ -253,7 +269,13 @@
                 send(cols_in.at[it, 0], cols_in.at[it, r], col_phase, col_ids[r])
 
         if it == ITERS - 1:
-            sums_phase = next(phases)
+            sums_phases = next(phases), next(phases)
+
+            def send_sums(half, peers):
+                for r in peers:
+                    part = sums_out.at[col_peers[r][1], pl.ds(half * QUARTER, QUARTER)]
+                    send(part, sums_in.at[half, r], sums_phases[half], col_ids[r])
+
             for step in reversed(steps):
                 at = lax.rem(ya + step, AY)
 
@@ -274,10 +296,10 @@
                     pair = turned[:, h * LANES : (h + 1) * LANES].T
                     sums_out[at * AZ + 2 * h] = pair[:HALF]
                     sums_out[at * AZ + 2 * h + 1] = pair[HALF:]
-                for r in far_first:
-                    if r and r // AZ == step:
-                        send(sums_out.at[col_peers[r][1]], sums_in.at[r], sums_phase, col_ids[r])
-            sums_in[0] = sums_out[mine_a]
+                send_sums(0, [r for r in far_first if r and r // AZ == step])
+            send_sums(1, far_first[:-1])
+            for half in range(2):
+                sums_in[half, 0] = sums_out[mine_a, half * QUARTER : (half + 1) * QUARTER]
 
         arrived(cols_in.at[it, pl.ds(1, NA - 1)], col_phase)
         scales = col_mass / jnp.sum(cols_in[it], axis=0)
@@ -295,17 +317,19 @@
 
     lax.fori_loop(0, NB, plan_rows, 0, unroll=many)
 
-    arrived(sums_in.at[pl.ds(1, NA - 1)], sums_phase)
-    new_own = normalized_rows(jnp.sum(sums_in[...], axis=0))
-    news[mine_a] = new_own.astype(jnp.bfloat16)
     new_phases = [next(phases) for _ in range(AY)]
-    for r in far_first:
-        if r:
-            send(news.at[mine_a], news.at[mine_a], new_phases[r // AZ], col_ids[r])
-    new_ref[...] = new_own
+    for half in range(2):
+        arrived(sums_in.at[half, pl.ds(1, NA - 1)], sums_phases[half])
+        new_own = normalized_rows(jnp.sum(sums_in[half], axis=0))
+        place = pl.ds(half * QUARTER, QUARTER)
+        news[mine_a, place] = new_own.astype(jnp.bfloat16)
+        for r in far_first[:-1]:
+            send(news.at[mine_a, place], news.at[mine_a, place], new_phases[r // AZ], col_ids[r])
+        new_ref[place, :] = new_own
 
     chunk = max(NB // SOFT_CHUNKS, 1)
     soft_phases = []
+    firsts = [step * chunk for step in reversed(nearest_first(NB // chunk))]
     for order, step in enumerate(steps):
         at = panel_at[step]
         arrived(news.at[pl.ds(0, AZ - (step == 0))], new_phases[step])
@@ -322,7 +346,7 @@
 
             lax.fori_loop(0, NB // many, soft_rows, 0)
             continue
-        for first in range(0, NB, chunk):
+        for first in firsts:
             block = jnp.dot(
                 jnp.concatenate([half_mat[at, row_peers[r][1]] for r in range(first, first + chunk)], axis=0),
                 fresh,
@@ -336,9 +360,9 @@
             soft_phases.append(phase)
             send(soft.at[1 - core, pl.ds(first, chunk)], soft_pair.at[pl.ds(first, chunk)], phase, sibling)
     soft_phase = next(phases)
-    for first, phase in zip(range(0, NB, chunk), soft_phases):
+    for first, phase in zip(firsts, soft_phases):
         arrived(soft_pair.at[pl.ds(first, chunk)], phase)
-        for r in range(first, first + chunk):
+        for r in reversed(range(first, first + chunk)):
             if r == 0:
                 soft_in[0] = soft[core, 0] + soft_pair[0]
             else:
@@ -379,15 +403,15 @@
         pltpu.VMEM((ITERS, NA, groups, LANES), f32),
         pltpu.VMEM((AY, NB, LANES, panel), bf16),
         pltpu.VMEM((NA, HALF, LANES), f32),
-        pltpu.VMEM((NA, HALF, LANES), f32),
+        pltpu.VMEM((2, NA, QUARTER, LANES), f32),
         pltpu.VMEM((NA, HALF, LANES), bf16),
         pltpu.VMEM((2, NB, HALF, LANES), f32),
         pltpu.VMEM((NB, HALF, LANES), f32),
         pltpu.VMEM((NB, HALF, LANES), f32),
         pltpu.VMEM((NB, HALF, LANES), f32),
         pltpu.VMEM((2, HALF, LANES), f32),
-        pltpu.SemaphoreType.DMA((48,)),
-        pltpu.SemaphoreType.DMA((48,)),
+        pltpu.SemaphoreType.DMA((56,)),
+        pltpu.SemaphoreType.DMA((56,)),
         pltpu.SemaphoreType.DMA((2,)),
     ]
     return pl.pallas_call(

time: 111 us -> 106 us (0.955)
  Pallas kernels: 107 us -> 102 us
    pallas_call x1, Pallas kernels: 107 us -> 102 us  [shards(): pl.pallas_call(functools.partial(fused, dims), out_shape=(jax.ShapeDtypeS...]
where the time goes in v4:
time: 106 us; the launch traced here: 105 us
  Pallas kernels  102 us (96%)
  local copies, waits for them, and re-layouts  2.82 us (3%)
    pallas_call x1, Pallas kernels, shards(): pl.pallas_call(functools.partial(fused, dims), out_shape=(jax.ShapeDtypeS...  102 us
    unnamed x6, local copies, waits for them, and re-layouts  2.82 us

profile of v4, /device:TPU:1, one launch (start us, length us, event | category | flops | bytes accessed | tf_op | source)
XLA Modules:
  0.0 105.3 jit_solution(5731383819569560257)
XLA Ops:
  0.6 0.0 copy-start
  0.6 0.8 copy-done
  1.5 0.0 copy-start.1
  1.5 0.8 copy-done.1
  2.2 101.9 %kmeans_step.1 = (f32[64,128]{1,0:T(8,128)S(1)}, f32[120,128]{1,0:T(8,128)S(1)}) custom-call(f32[120,128]{1,0:T(8,128)S(1)} %copy-done, f32[64,128]{1,0:T(8,128)S(1)} %copy-done.1), custom_call_target="tpu_custom_call" | custom-call | tf_op jit(solution)/shard_map/kmeans_step/pallas_call | solution.py:417
  104.1 0.6 copy.6
  104.7 0.6 copy.7
Async XLA Ops:
  0.6 0.8 copy-start
  1.5 0.8 copy-start.1

commit v5 on v4

--- a/solution.py
+++ b/solution.py
@@ -14,6 +14,8 @@
 LANES = 128
 HALF = 64
 QUARTER = 32
+PART = 16
+PARTS = HALF // PART
 SOFT_CHUNKS = 4
 MESH = pl.DeviceIdType.MESH
 
@@ -82,7 +84,8 @@
     panel = AZ * HALF
     groups = NA * HALF // LANES
     per_panel = panel // LANES
-    many = min(NB, 4)
+    side = NB // 2
+    many = min(side, 4)
     col_mass = (rows_here * X * Y * Z) / (HALF * X * Y * Z * 2)
 
     dp = lax.axis_index("dp")
@@ -141,7 +144,7 @@
         pltpu.make_async_copy(view, view, recv_sem.at[phase]).wait()
         sent.append((view, phase))
 
-    phases = iter(range(56))
+    phases = iter(range(64))
 
     def slot(b):
         return jnp.concatenate([toks[0, b], toks[1, b]], axis=0)
@@ -182,6 +185,13 @@
     send(toks.at[core], toks.at[core], pair_phase, sibling)
     arrived(toks.at[0], pair_phase)
 
+    pair_rows_phases = []
+
+    def pair_rows(it, half):
+        view = pl.ds(half * side, side)
+        pair_rows_phases.append(next(phases))
+        send(rows_mine.at[it, view], rows_pair.at[it, view], pair_rows_phases[-1], sibling)
+
     slope = math.log2(math.e) / (SOFTMAX_WARMTH * LANES)
     offset = math.log2(math.e) / SOFTMAX_WARMTH
     for order, step in enumerate(steps):
@@ -212,13 +222,18 @@
                     rows_mine[0, pl.ds(first + j, 1), :] = jnp.sum(total.T, axis=0, keepdims=True)
             return carry
 
-        lax.fori_loop(0, NB // many, kernel_rows, 0)
+        lax.fori_loop(0, side // many, kernel_rows, 0)
+        if order == AY - 1:
+            pair_rows(0, 0)
+        lax.fori_loop(side // many, NB // many, kernel_rows, 0)
+        if order == AY - 1:
+            pair_rows(0, 1)
 
     def part_of(b, g):
         h = g % per_panel
         return kern[g // per_panel, b, :, h * LANES : (h + 1) * LANES]
 
-    valid = lax.broadcasted_iota(jnp.int32, (NB, LANES), 1) < rows_here
+    valid = lax.broadcasted_iota(jnp.int32, (side, LANES), 1) < rows_here
     scales = None
     for it in range(ITERS):
         if it:
@@ -231,15 +246,17 @@
                 rows_mine[it, pl.ds(b, 1), :] = jnp.sum(total.T, axis=0, keepdims=True)
                 return carry
 
-            lax.fori_loop(0, NB, scaled_rows, 0, unroll=many)
-
-        phase = next(phases)
-        send(rows_mine.at[it], rows_pair.at[it], phase, sibling)
-        arrived(rows_pair.at[it], phase)
-        rows_in[it, 0] = rows_mine[it] + rows_pair[it]
-        phase = next(phases)
-        for r in row_far[:-1]:
-            send(rows_in.at[it, 0], rows_in.at[it, r], phase, row_ids[r])
+            for half in range(2):
+                lax.fori_loop(half * side, half * side + side, scaled_rows, 0, unroll=many)
+                pair_rows(it, half)
+
+        rows_phases = next(phases), next(phases)
+        for half in range(2):
+            view = pl.ds(half * side, side)
+            arrived(rows_pair.at[it, view], pair_rows_phases[2 * it + half])
+            rows_in[it, half, 0] = rows_mine[it, view] + rows_pair[it, view]
+            for r in row_far[:-1]:
+                send(rows_in.at[it, half, 0], rows_in.at[it, half, r], rows_phases[half], row_ids[r])
         if it == 0:
             def turn(b, carry):
                 place = pl.ds(pl.multiple_of(b * LANES, LANES), LANES)
@@ -247,10 +264,6 @@
                 return carry
 
             lax.fori_loop(0, NB, turn, 0, unroll=many)
-        arrived(rows_in.at[it, pl.ds(1, NB - 1)], phase)
-        row_sum = jnp.sum(rows_in[it], axis=0)
-        weights[...] = jnp.where(valid, 1.0 / row_sum, 0.0)
-
         def weighted_columns(b, totals):
             spread = jnp.broadcast_to(weights[pl.ds(b, 1), :], (LANES, LANES)).T
             weight_cols[b] = spread
@@ -260,7 +273,12 @@
             )
 
         zeros = tuple(jnp.zeros((8, LANES), jnp.float32) for _ in range(groups))
-        totals = lax.fori_loop(0, NB, weighted_columns, zeros, unroll=many)
+        totals = zeros
+        for half in range(2):
+            arrived(rows_in.at[it, half, pl.ds(1, NB - 1)], rows_phases[half])
+            row_sum = jnp.sum(rows_in[it, half], axis=0)
+            weights[pl.ds(half * side, side), :] = jnp.where(valid, 1.0 / row_sum, 0.0)
+            totals = lax.fori_loop(half * side, half * side + side, weighted_columns, totals, unroll=many)
         for g in range(groups):
             cols_in[it, 0, g : g + 1, :] = jnp.sum(totals[g], axis=0, keepdims=True)
         col_phase = next(phases)
@@ -269,11 +287,11 @@
                 send(cols_in.at[it, 0], cols_in.at[it, r], col_phase, col_ids[r])
 
         if it == ITERS - 1:
-            sums_phases = next(phases), next(phases)
+            sums_phases = [next(phases) for _ in range(PARTS)]
 
             def send_sums(half, peers):
                 for r in peers:
-                    part = sums_out.at[col_peers[r][1], pl.ds(half * QUARTER, QUARTER)]
+                    part = sums_out.at[col_peers[r][1], pl.ds(half * PART, PART)]
                     send(part, sums_in.at[half, r], sums_phases[half], col_ids[r])
 
             for step in reversed(steps):
@@ -297,9 +315,10 @@
                     sums_out[at * AZ + 2 * h] = pair[:HALF]
                     sums_out[at * AZ + 2 * h + 1] = pair[HALF:]
                 send_sums(0, [r for r in far_first if r and r // AZ == step])
-            send_sums(1, far_first[:-1])
-            for half in range(2):
-                sums_in[half, 0] = sums_out[mine_a, half * QUARTER : (half + 1) * QUARTER]
+            for half in range(1, PARTS):
+                send_sums(half, far_first[:-1])
+            for half in range(PARTS):
+                sums_in[half, 0] = sums_out[mine_a, half * PART : (half + 1) * PART]
 
         arrived(cols_in.at[it, pl.ds(1, NA - 1)], col_phase)
         scales = col_mass / jnp.sum(cols_in[it], axis=0)
@@ -318,10 +337,10 @@
     lax.fori_loop(0, NB, plan_rows, 0, unroll=many)
 
     new_phases = [next(phases) for _ in range(AY)]
-    for half in range(2):
+    for half in range(PARTS):
         arrived(sums_in.at[half, pl.ds(1, NA - 1)], sums_phases[half])
         new_own = normalized_rows(jnp.sum(sums_in[half], axis=0))
-        place = pl.ds(half * QUARTER, QUARTER)
+        place = pl.ds(half * PART, PART)
         news[mine_a, place] = new_own.astype(jnp.bfloat16)
         for r in far_first[:-1]:
             send(news.at[mine_a, place], news.at[mine_a, place], new_phases[r // AZ], col_ids[r])
@@ -346,6 +365,17 @@
 
             lax.fori_loop(0, NB // many, soft_rows, 0)
             continue
+        soft_phase = next(phases)
+
+        def pass_on(first, phase):
+            arrived(soft_pair.at[pl.ds(first, chunk)], phase)
+            for r in reversed(range(first, first + chunk)):
+                if r == 0:
+                    soft_in[0] = soft[core, 0] + soft_pair[0]
+                else:
+                    soft_half[r] = soft[core, r] + soft_pair[r]
+                    send(soft_half.at[r], soft_in.at[r], soft_phase, row_ids[r])
+
         for first in firsts:
             block = jnp.dot(
                 jnp.concatenate([half_mat[at, row_peers[r][1]] for r in range(first, first + chunk)], axis=0),
@@ -356,18 +386,16 @@
                 whole = block[(r - first) * LANES : (r - first + 1) * LANES] + tile_acc[row_peers[r][1]]
                 soft[0, r] = whole[:HALF]
                 soft[1, r] = whole[HALF:]
-            phase = next(phases)
-            soft_phases.append(phase)
-            send(soft.at[1 - core, pl.ds(first, chunk)], soft_pair.at[pl.ds(first, chunk)], phase, sibling)
-    soft_phase = next(phases)
-    for first, phase in zip(firsts, soft_phases):
-        arrived(soft_pair.at[pl.ds(first, chunk)], phase)
-        for r in reversed(range(first, first + chunk)):
-            if r == 0:
-                soft_in[0] = soft[core, 0] + soft_pair[0]
-            else:
-                soft_half[r] = soft[core, r] + soft_pair[r]
-                send(soft_half.at[r], soft_in.at[r], soft_phase, row_ids[r])
+            soft_phases.append((first, next(phases)))
+            send(
+                soft.at[1 - core, pl.ds(first, chunk)],
+                soft_pair.at[pl.ds(first, chunk)],
+                soft_phases[-1][1],
+                sibling,
+            )
+            if len(soft_phases) > 1:
+                pass_on(*soft_phases[-2])
+        pass_on(*soft_phases[-1])
     arrived(soft_in.at[pl.ds(1, NB - 1)], soft_phase)
     soft_fin[core] = jnp.sum(soft_in[...], axis=0)
     phase = next(phases)
@@ -397,21 +425,21 @@
         pltpu.VMEM((NB, LANES, LANES), f32),
         pltpu.VMEM((ITERS, NB, LANES), f32),
         pltpu.VMEM((ITERS, NB, LANES), f32),
-        pltpu.VMEM((ITERS, NB, NB, LANES), f32),
+        pltpu.VMEM((ITERS, 2, NB, NB // 2, LANES), f32),
         pltpu.VMEM((NB, LANES), f32),
         pltpu.VMEM((NB, LANES, LANES), f32),
         pltpu.VMEM((ITERS, NA, groups, LANES), f32),
         pltpu.VMEM((AY, NB, LANES, panel), bf16),
         pltpu.VMEM((NA, HALF, LANES), f32),
-        pltpu.VMEM((2, NA, QUARTER, LANES), f32),
+        pltpu.VMEM((PARTS, NA, PART, LANES), f32),
         pltpu.VMEM((NA, HALF, LANES), bf16),
         pltpu.VMEM((2, NB, HALF, LANES), f32),
         pltpu.VMEM((NB, HALF, LANES), f32),
         pltpu.VMEM((NB, HALF, LANES), f32),
         pltpu.VMEM((NB, HALF, LANES), f32),
         pltpu.VMEM((2, HALF, LANES), f32),
-        pltpu.SemaphoreType.DMA((56,)),
-        pltpu.SemaphoreType.DMA((56,)),
+        pltpu.SemaphoreType.DMA((64,)),
+        pltpu.SemaphoreType.DMA((64,)),
         pltpu.SemaphoreType.DMA((2,)),
     ]
     return pl.pallas_call(

time: 106 us -> 105 us (level)
    pallas_call x1, Pallas kernels: 102 us -> 101 us  [shards(): pl.pallas_call(functools.partial(fused, dims), out_shape=(jax.ShapeDtypeS...]
where the time goes in v5:
time: 105 us; the launch traced here: 104 us
  Pallas kernels  101 us (96%)
  local copies, waits for them, and re-layouts  2.82 us (3%)
    pallas_call x1, Pallas kernels, shards(): pl.pallas_call(functools.partial(fused, dims), out_shape=(jax.ShapeDtypeS...  101 us
    unnamed x6, local copies, waits for them, and re-layouts  2.82 us

profile of v5, /device:TPU:1, one launch (start us, length us, event | category | flops | bytes accessed | tf_op | source)
XLA Modules:
  0.0 104.3 jit_solution(4379448910075816340)
XLA Ops:
  0.6 0.0 copy-start
  0.6 0.8 copy-done
  1.5 0.0 copy-start.1
  1.5 0.8 copy-done.1
  2.2 100.8 %kmeans_step.1 = (f32[64,128]{1,0:T(8,128)S(1)}, f32[120,128]{1,0:T(8,128)S(1)}) custom-call(f32[120,128]{1,0:T(8,128)S(1)} %copy-done, f32[64,128]{1,0:T(8,128)S(1)} %copy-done.1), custom_call_target="tpu_custom_call" | custom-call | tf_op jit(solution)/shard_map/kmeans_step/pallas_call | solution.py:445
  103.0 0.6 copy.6
  103.6 0.6 copy.7
Async XLA Ops:
  0.6 0.8 copy-start
  1.5 0.8 copy-start.1

commit v6 on v5

--- a/solution.py
+++ b/solution.py
@@ -282,8 +282,8 @@
         for g in range(groups):
             cols_in[it, 0, g : g + 1, :] = jnp.sum(totals[g], axis=0, keepdims=True)
         col_phase = next(phases)
-        for r in far_first:
-            if r:
+        if it < ITERS - 1:
+            for r in far_first[:-1]:
                 send(cols_in.at[it, 0], cols_in.at[it, r], col_phase, col_ids[r])
 
         if it == ITERS - 1:
@@ -315,6 +315,8 @@
                     sums_out[at * AZ + 2 * h] = pair[:HALF]
                     sums_out[at * AZ + 2 * h + 1] = pair[HALF:]
                 send_sums(0, [r for r in far_first if r and r // AZ == step])
+            for r in far_first[:-1]:
+                send(cols_in.at[it, 0], cols_in.at[it, r], col_phase, col_ids[r])
             for half in range(1, PARTS):
                 send_sums(half, far_first[:-1])
             for half in range(PARTS):

time: 105 us -> 104 us (level)
  no operation moved by 1% of the time
where the time goes in v6:
time: 104 us
  Pallas kernels  101 us (97%)
  local copies, waits for them, and re-layouts  2.82 us (3%)
    pallas_call x1, Pallas kernels, shards(): pl.pallas_call(functools.partial(fused, dims), out_shape=(jax.ShapeDtypeS...  101 us
    unnamed x6, local copies, waits for them, and re-layouts  2.82 us

profile of v6, /device:TPU:1, one launch (start us, length us, event | category | flops | bytes accessed | tf_op | source)
XLA Modules:
  0.0 104.2 jit_solution(16265626189730670730)
XLA Ops:
  0.6 0.0 copy-start
  0.6 0.8 copy-done
  1.5 0.0 copy-start.1
  1.5 0.8 copy-done.1
  2.2 100.8 %kmeans_step.1 = (f32[64,128]{1,0:T(8,128)S(1)}, f32[120,128]{1,0:T(8,128)S(1)}) custom-call(f32[120,128]{1,0:T(8,128)S(1)} %copy-done, f32[64,128]{1,0:T(8,128)S(1)} %copy-done.1), custom_call_target="tpu_custom_call" | custom-call | tf_op jit(solution)/shard_map/kmeans_step/pallas_call | solution.py:447
  103.0 0.6 copy.6
  103.6 0.6 copy.7
Async XLA Ops:
  0.6 0.8 copy-start
  1.5 0.8 copy-start.1
